TPU v7x, 32 devices: a whole 2x2x4 slice. The times are simulated.
32 devices in a mesh: ctx: 8 (over z, x), head: 4 (over y, core).
Axes of the slice: x: 2, y: 2, z: 4, core: 2. Of those that a mesh axis runs over, the one named last changes fastest.
Arguments:
- queries: bfloat16 [2048, 2048], P('ctx', 'head'), may hold values from -110 to 110
- keys: bfloat16 [32768, 128], P('ctx'), may hold values from -6 to 6
- values: bfloat16 [32768, 128], P('ctx'), may hold values from -6 to 6
- w_out: bfloat16 [2048, 16384], P(None, 'head'), may hold values from -0.125 to 0.125
- new_counts: int32 [8], replicated, may hold values from 1 to 1024, as said below
- prior_lengths: int32 [8], replicated, may hold values from 1 to 15360, as said below
Outputs:
- mixed: bfloat16 [2048, 16384], P('ctx', 'head')
Inputs may be any that keep to these rules, and one draw needn't show every extreme that they name: `new_counts`: every request has at least one new token; the counts add up to 2048. `prior_lengths`: every request has at least one cached token; the lengths add up to 30720.
All inputs are finite; a program needn't handle non-finite values.
Results may differ from a plain program's by a relative error of at most 0.011.
Values may be sent and summed in bfloat16 or wider, within the bound.
No kernel may reach another device: no remote copies, remote signals or barrier semaphores. Data moves between devices by JAX's collectives and lax.ppermute only.
A program may use at most 384 MiB of HBM per device.

v0:
```python
import functools
import math

import jax
import jax.numpy as jnp
from jax import lax
from jax.experimental import pallas as pl
from jax.experimental.pallas import tpu as pltpu
from jax.sharding import PartitionSpec as P

NEG = -1e30
CALM = 60.0
KEY_TILE = 512
FEW_ROWS = 64
SIDE = 16
LANES = 128
STRETCHES = 3
MIB = 1024 * 1024
SMEM = pl.BlockSpec(memory_space=pltpu.SMEM)
VMEM = pl.BlockSpec(memory_space=pltpu.VMEM)
HBM = pl.BlockSpec(memory_space=pltpu.HBM)


def lengths(rows):
    wide = rows.astype(jnp.float32)
    return jnp.sum(wide * wide, axis=1, keepdims=True)


def fill(from_keys, from_values, done, keys_ref, beside_ref):
    count, width = from_keys.shape
    step = min(KEY_TILE, count)

    def turn(at, longest):
        here = pl.ds(pl.multiple_of(at * step, step), step)
        there = pl.ds(pl.multiple_of(done + at * step, step), step)
        keys = from_keys[here, :]
        keys_ref[there, :] = keys
        beside_ref[there, :width] = from_values[here, :]
        beside_ref[there, width:] = jnp.ones((step, width), jnp.bfloat16)
        return jnp.maximum(longest, lengths(keys))

    return jnp.max(lax.fori_loop(0, count // step, turn, jnp.zeros((step, 1), jnp.float32)))


def prepare_kernel(keys_ref, values_ref, far_w, all_keys, beside_ref, longest_ref, near_w, sem):
    fetch = pltpu.make_async_copy(far_w, near_w, sem)
    fetch.start()
    longest_ref[0] = fill(keys_ref, values_ref, 0, all_keys, beside_ref)
    fetch.wait()


def prepare(keys, values, w_out):
    cache, width = keys.shape
    return pl.pallas_call(
        prepare_kernel,
        out_shape=(
            pltpu.VMEM((2 * cache, width), jnp.bfloat16),
            pltpu.VMEM((2 * cache, 2 * width), jnp.bfloat16),
            jax.ShapeDtypeStruct((1,), jnp.float32),
            pltpu.VMEM(w_out.shape, w_out.dtype),
        ),
        in_specs=[VMEM, VMEM, HBM],
        out_specs=(VMEM, VMEM, SMEM, VMEM),
        scratch_shapes=[pltpu.SemaphoreType.DMA],
        compiler_params=pltpu.CompilerParams(vmem_limit_bytes=4 * MIB),
        name="prepare",
    )(keys, values, pltpu.with_memory_space_constraint(w_out, pltpu.HBM))


def stack_kernel(slots, group_at, width, plan_ref, *refs):
    q_refs, (stack_ref, longest_ref, q_all, sems) = refs[:slots], refs[slots:]
    rows = q_refs[0].shape[0]
    heads = q_refs[0].shape[1] // width
    local = slots * rows
    copies = [pltpu.make_async_copy(q_ref, q_all.at[slot], sems.at[slot]) for slot, q_ref in enumerate(q_refs)]
    for copy in copies:
        copy.start()
    longest = jnp.zeros((rows, 1), jnp.float32)
    for slot, copy in enumerate(copies):
        copy.wait()
        start = plan_ref[group_at + slot] * rows
        for head in range(heads):
            part = q_all[slot, :, head * width:(head + 1) * width]
            stack_ref[pl.ds(pl.multiple_of(head * local + start, rows), rows), :] = part
            longest = jnp.maximum(longest, lengths(part))
    longest_ref[0] = jnp.max(longest)


def stack_queries(places, plan, queries, width):
    slots, (rows, wide) = len(queries), queries[0].shape
    return pl.pallas_call(
        functools.partial(stack_kernel, slots, places["groups"], width),
        out_shape=(
            pltpu.VMEM((slots * rows * (wide // width), width), jnp.bfloat16),
            jax.ShapeDtypeStruct((1,), jnp.float32),
        ),
        in_specs=[SMEM] + [HBM] * slots,
        out_specs=(VMEM, SMEM),
        scratch_shapes=[pltpu.VMEM((slots, rows, wide), jnp.bfloat16), pltpu.SemaphoreType.DMA((slots,))],
        compiler_params=pltpu.CompilerParams(vmem_limit_bytes=4 * MIB),
        name="stack",
    )(plan, *queries)


def request_table(new_ref, prior_ref):
    table = []
    row, key = jnp.int32(0), jnp.int32(0)
    for request in range(new_ref.shape[0]):
        new, prior = new_ref[request], prior_ref[request]
        table.append((row, key, key + prior - row, row + new, key + new + prior))
        row, key = row + new, key + new + prior
    return table


def key_range(table, row):
    first, shift = table[0][1], table[0][2]
    for start, key, ahead, _, _ in table[1:]:
        own = row >= start
        first = jnp.where(own, key, first)
        shift = jnp.where(own, ahead, shift)
    return first, row + shift


def attend_kernel(shape, places, *refs):
    groups, rows, heads, requests = shape
    plan_ref, key_norm_ref, query_norm_ref, stack_ref = refs[:4]
    fetched = refs[4:6]
    keys_ref, beside_ref = refs[8:10]
    out_refs = refs[10:10 + groups]
    sums, tops, chunk_q, chunk_sum, chunk_top, arrived, sems = refs[10 + groups:]
    cache, width = keys_ref.shape[0] // 2, keys_ref.shape[1]
    local = groups * rows
    step = min(KEY_TILE, cache // 2)
    scale = width ** (-0.5)
    factor = scale * math.log2(math.e)
    copies = [pltpu.make_async_copy(ref, arrived.at[at], sems.at[at]) for at, ref in enumerate(fetched)]
    for copy in copies:
        copy.start()
    key_norm = key_norm_ref[0]
    for at, copy in enumerate(copies):
        copy.wait()
        part = arrived.at[at]
        longest = fill(part.at[:, :width], part.at[:, width:], cache + at * (cache // 2), keys_ref, beside_ref)
        key_norm = jnp.maximum(key_norm, longest)
    calm = key_norm * query_norm_ref[0] * (scale * scale) <= CALM * CALM
    side = plan_ref[places["side"]]

    def clear(at, carry):
        sums[pl.ds(pl.multiple_of(at * rows, rows), rows), :] = jnp.zeros((rows, 2 * width), jnp.float32)
        return carry

    lax.fori_loop(0, heads * groups, clear, 0)

    def global_row(place):
        whole = place + side * rows
        for group in range(1, groups):
            whole = whole + jnp.where(place >= group * rows, rows, 0)
        return whole

    def one_chunk(count, online, request, begin, end, start):
        first_key = plan_ref[places["first_key"] + request]
        ahead = plan_ref[places["ahead"] + request]
        start = pl.multiple_of(start, SIDE)
        low_key, high_key = global_row(begin) + ahead, global_row(end - 1) + ahead
        total = heads * count
        for head in range(heads):
            chunk_q[head * count:(head + 1) * count, :] = stack_ref[
                pl.ds(pl.multiple_of(head * local + start, SIDE), count), :
            ]
        chunk_sum[:total, :] = jnp.zeros((total, 2 * width), jnp.float32)
        if online:
            chunk_top[:total, :] = jnp.full((total, width), NEG, jnp.float32)
        place = start + lax.broadcasted_iota(jnp.int32, (count, 1), 0)
        last = global_row(place) + ahead

        def scores(part, left):
            return lax.dot_general(
                chunk_q[part, :], keys_ref[pl.ds(left, step), :], (((1,), (1,)), ((), ())),
                preferred_element_type=jnp.float32,
            ) * factor

        def add(left, weights):
            return jnp.dot(
                weights.astype(jnp.bfloat16), beside_ref[pl.ds(left, step), :], preferred_element_type=jnp.float32
            )

        def one_step(left, key):
            def allowed():
                index = key + lax.broadcasted_iota(jnp.int32, (count, step), 1)
                return (index >= first_key) & (index <= last)

            if online:
                mask = allowed()

                def one_head(head, carry):
                    part = pl.ds(pl.multiple_of(head * count, count), count)
                    score = jnp.where(mask, scores(part, left), NEG)
                    old = chunk_top[part, :]
                    new = jnp.maximum(old, jnp.ceil(jnp.max(score, axis=1, keepdims=True)))
                    weights = jnp.where(mask, jnp.exp2(score - new[:, :1]), 0.0)
                    shrink = jnp.exp2(old - new)
                    chunk_sum[part, :width] = chunk_sum[part, :width] * shrink
                    chunk_sum[part, width:] = chunk_sum[part, width:] * shrink
                    chunk_sum[part, :] += add(left, weights)
                    chunk_top[part, :] = new
                    return carry

                lax.fori_loop(0, heads, one_head, 0)
                return

            plain = (key >= first_key) & (key + step - 1 <= low_key)

            @pl.when(plain)
            def _():
                for head in range(heads):
                    part = pl.ds(head * count, count)
                    chunk_sum[part, :] += add(left, jnp.exp2(scores(part, left)))

            @pl.when(jnp.logical_not(plain))
            def _():
                mask = allowed()
                weights = jnp.exp2(scores(pl.ds(0, total), left))
                weights = jnp.concatenate([
                    jnp.where(mask, weights[head * count:(head + 1) * count, :], 0.0) for head in range(heads)
                ])
                chunk_sum[:total, :] += add(left, weights)

        def one_part(part, carry):
            left, key, steps = (plan_ref[places[name] + part] for name in ("lefts", "keys", "steps"))
            low = jnp.clip(lax.div(first_key - key, step), 0, steps)
            high = jnp.clip(lax.div(high_key - key + step, step), 0, steps)

            def turn(at, carry):
                one_step(pl.multiple_of(left + at * step, step), key + at * step)
                return carry

            lax.fori_loop(low, high, turn, 0)
            return carry

        lax.fori_loop(0, STRETCHES, one_part, 0)
        own = (place >= begin) & (place < end)
        for head in range(heads):
            here = pl.ds(pl.multiple_of(head * local + start, SIDE), count)
            part = slice(head * count, (head + 1) * count)
            sums[here, :] += jnp.where(own, chunk_sum[part, :], 0.0)
            if online:
                tops[here, :] = jnp.where(own, chunk_top[part, :], tops[here, :])

    def all_chunks(count, online, request, begin, end):
        aligned = lax.div(begin, SIDE) * SIDE

        def turn(at, carry):
            from_row = aligned + at * count
            one_chunk(
                count,
                online,
                request,
                jnp.maximum(begin, from_row),
                jnp.minimum(end, from_row + count),
                jnp.minimum(from_row, local - count),
            )
            return carry

        lax.fori_loop(0, lax.div(end - aligned + (count - 1), count), turn, 0)

    many, few = min(2 * rows + SIDE, local), min(FEW_ROWS, local)

    def one_request(request, carry):
        begin, end = plan_ref[places["begin"] + request], plan_ref[places["end"] + request]
        large = end - lax.div(begin, SIDE) * SIDE > 2 * few

        @pl.when((end > begin) & calm & large)
        def _():
            all_chunks(many, False, request, begin, end)

        @pl.when((end > begin) & calm & jnp.logical_not(large))
        def _():
            all_chunks(few, False, request, begin, end)

        @pl.when((end > begin) & jnp.logical_not(calm))
        def _():
            all_chunks(few, True, request, begin, end)

        return carry

    lax.fori_loop(0, requests, one_request, 0)

    lane = lax.broadcasted_iota(jnp.int32, (LANES, LANES), 1)
    for slot, out_ref in enumerate(out_refs):
        start = plan_ref[places["groups"] + slot] * rows
        out_ref[rows:, :] = jnp.zeros((SIDE, heads * width), jnp.bfloat16)
        for at in range(0, rows, LANES):
            terms = jnp.zeros((LANES, LANES), jnp.float32)
            for head in range(heads):
                here = pl.ds(pl.multiple_of(head * local + start + at, LANES), LANES)
                out_ref[at:at + LANES, head * width:(head + 1) * width] = sums[here, :width].astype(jnp.bfloat16)
                weight = sums[here, width:]
                top = jnp.where(weight > 0.0, jnp.where(calm, 0.0, tops[here, :]), NEG)
                for term, value in enumerate((weight, top)):
                    high = value.astype(jnp.bfloat16).astype(jnp.float32)
                    terms = jnp.where(lane == 2 * term * heads + head, high, terms)
                    terms = jnp.where(lane == (2 * term + 1) * heads + head, value - high, terms)
            out_ref[rows:, at:at + LANES] = terms.T[:SIDE, :].astype(jnp.bfloat16)


def attend(places, plan, norms, stack, fetched, all_keys, beside, shape):
    groups, rows, heads, _ = shape
    cache, width = all_keys.shape[0] // 2, all_keys.shape[1]
    local = groups * rows
    most = heads * min(2 * rows + SIDE, local)
    _, _, *payloads = pl.pallas_call(
        functools.partial(attend_kernel, shape, dict(places)),
        out_shape=(pltpu.VMEM(all_keys.shape, all_keys.dtype), pltpu.VMEM(beside.shape, beside.dtype))
        + (jax.ShapeDtypeStruct((rows + SIDE, heads * width), jnp.bfloat16),) * groups,
        in_specs=[SMEM] * 3 + [VMEM] + [HBM] * 2 + [VMEM] * 2,
        out_specs=(VMEM,) * (groups + 2),
        input_output_aliases={6: 0, 7: 1},
        scratch_shapes=[
            pltpu.VMEM((heads * local, 2 * width), jnp.float32),
            pltpu.VMEM((heads * local, width), jnp.float32),
            pltpu.VMEM((most, width), jnp.bfloat16),
            pltpu.VMEM((most, 2 * width), jnp.float32),
            pltpu.VMEM((heads * min(FEW_ROWS, local), width), jnp.float32),
            pltpu.VMEM((2, cache // 2, 2 * width), jnp.bfloat16),
            pltpu.SemaphoreType.DMA((2,)),
        ],
        compiler_params=pltpu.CompilerParams(vmem_limit_bytes=28 * MIB),
        cost_estimate=pl.CostEstimate(
            flops=local * heads * cache * width * 4, bytes_accessed=24 * MIB, transcendentals=0
        ),
        name="attend",
    )(plan, *norms, stack, *fetched, all_keys, beside)
    return payloads


def merge_kernel(heads, there_at, plan_ref, *refs):
    parts, out_ref = refs[:-1], refs[-1]
    rows = out_ref.shape[0]
    width = out_ref.shape[1] // heads
    logs = [
        jnp.where(plan_ref[there_at + at] == 1, part[rows:, :rows].astype(jnp.float32), 0.0) for at, part in enumerate(parts)
    ]
    spare = LANES - SIDE * len(parts)
    if spare:
        logs.append(jnp.zeros((spare, rows), jnp.float32))
    terms = jnp.concatenate(logs, axis=0).T
    total = terms + pltpu.roll(terms, LANES - heads, 1)
    top = pltpu.roll(terms, LANES - 2 * heads, 1) + pltpu.roll(terms, LANES - 3 * heads, 1)
    lane = lax.broadcasted_iota(jnp.int32, (rows, LANES), 1)
    used = (lax.rem(lane, SIDE) < heads) & (lane < SIDE * len(parts)) & (total > 0.0)
    top = jnp.where(used, top, NEG)
    biggest = top
    for shift in (16, 32, 64):
        biggest = jnp.maximum(biggest, pltpu.roll(biggest, shift, 1))
    share = jnp.where(used, jnp.exp2(top - biggest), 0.0)
    weight = share * jnp.where(used, total, 0.0)
    for shift in (16, 32, 64):
        weight = weight + pltpu.roll(weight, shift, 1)
    share = share / weight
    for head in range(heads):
        own = slice(head * width, (head + 1) * width)
        mixed = jnp.zeros((rows, width), jnp.float32)
        for at, part in enumerate(parts):
            lane_at = at * SIDE + head
            mixed = mixed + part[:rows, own].astype(jnp.float32) * share[:, lane_at:lane_at + 1]
        out_ref[:, own] = mixed.astype(out_ref.dtype)


def merge(places, plan, parts, heads):
    rows = parts[0].shape[0] - SIDE
    return pl.pallas_call(
        functools.partial(merge_kernel, heads, places["there"]),
        out_shape=jax.ShapeDtypeStruct((rows, parts[0].shape[1]), jnp.bfloat16),
        in_specs=[SMEM] + [VMEM] * len(parts),
        out_specs=VMEM,
        compiler_params=pltpu.CompilerParams(vmem_limit_bytes=12 * MIB),
        name="merge",
    )(plan, *parts)


def project_kernel(order, going_on, last, from_at, plan_ref, *refs):
    refs = list(refs)
    before_ref = refs.pop(0) if going_on else None
    piece_refs, (w_ref, out_ref, token_ref) = refs[:len(order)], refs[len(order):]
    deep = piece_refs[0].shape[1]
    block = out_ref.shape[1]
    left = pl.multiple_of(pl.program_id(0) * block, block)
    token_ref[0] = jnp.int32(0)
    total = None
    for at, piece_ref in zip(order, piece_refs):
        own = pl.multiple_of(plan_ref[from_at + at] * deep, deep)
        term = jnp.dot(
            piece_ref[...], w_ref[pl.ds(own, deep), pl.ds(left, block)], preferred_element_type=jnp.float32
        )
        total = term if total is None else total + term
    if going_on:
        total = total + before_ref[:, pl.ds(left, block)]
    out_ref[...] = total.astype(out_ref.dtype)


def project(places, plan, order, pieces, w_out, before, last):
    rows, deep = pieces[0].shape
    depth, wide = w_out.shape
    block = min(1024, wide)
    going_on = before is not None
    return pl.pallas_call(
        functools.partial(project_kernel, order, going_on, last, places["from"]),
        out_shape=(
            pltpu.HBM((rows, wide), jnp.bfloat16) if last else pltpu.VMEM((rows, wide), jnp.float32),
            jax.ShapeDtypeStruct((1,), jnp.int32),
        ),
        grid=(wide // block,),
        in_specs=[SMEM] + [VMEM] * (going_on + len(pieces) + 1),
        out_specs=(pl.BlockSpec((rows, block), lambda at: (0, at)), SMEM),
        compiler_params=pltpu.CompilerParams(vmem_limit_bytes=16 * MIB),
        cost_estimate=pl.CostEstimate(
            flops=4 * rows * deep * len(pieces) * wide, bytes_accessed=2 * depth * wide, transcendentals=0
        ),
        name="project",
    )(plan, *([before] if going_on else []), *pieces, w_out)


def shift_pairs(count, stride, steps):
    groups = count // stride
    return [
        (group * stride + member, (group + steps) % groups * stride + member)
        for group in range(groups)
        for member in range(stride)
    ]


def swap_pairs(count):
    return [(at, at ^ 1) for at in range(count)]


def is_far(groups, one, two):
    low, high = min(one, two), max(one, two)
    return low < groups // 2 and high >= groups - max(1, groups // 4)


def move(value, groups, steps, far):
    pairs = [
        (source, target)
        for source, target in shift_pairs(2 * groups, 2, steps)
        if far or not is_far(groups, source // 2, target // 2)
    ]
    return lax.ppermute(value, "ctx", pairs) if pairs else jnp.zeros_like(value)


def plan_kernel(shape, places, new_ref, prior_ref, at_ref, plan_ref, far_ref):
    groups, chips, rows, cache, step = shape
    device, place = at_ref[0], at_ref[1]
    group, side, chip, core = lax.div(device, 2), lax.rem(device, 2), lax.div(place, 2), lax.rem(place, 2)
    table = request_table(new_ref, prior_ref)

    def rows_before(row):
        block = lax.div(row, rows)
        odd, inside = lax.rem(block, 2), lax.rem(row, rows)
        return lax.div(block, 2) * rows + jnp.where(odd == side, inside, jnp.where(odd == 1, rows, 0))

    for request, (row, key, ahead, row_end, _) in enumerate(table):
        plan_ref[places["first_key"] + request] = key
        plan_ref[places["ahead"] + request] = ahead
        plan_ref[places["begin"] + request] = rows_before(row)
        plan_ref[places["end"] + request] = rows_before(row_end)
    spans = [
        (key_range(table, jnp.int32(2 * rows * at))[0], key_range(table, jnp.int32(2 * rows * (at + 1) - 1))[1])
        for at in range(groups)
    ]
    needed = jnp.int32(0)
    for source in range(groups):
        for target in range(groups):
            if is_far(groups, source, target):
                first, last = spans[source]
                meet = (first < 2 * cache * (target + 1)) & (last >= 2 * cache * target)
                needed = jnp.where(meet, 1, needed)
    far_ref[0] = needed
    plan_ref[places["side"]] = side
    for steps in range(groups):
        plan_ref[places["groups"] + steps] = lax.rem(group + (groups - steps), groups)
        there = jnp.int32(1)
        for at in range(groups):
            if is_far(groups, (at + steps) % groups, at):
                there = jnp.where(group == at, needed, there)
        plan_ref[places["there"] + steps] = there
    other = (device + 1 - 2 * side) * cache
    half = cache // 2
    stretches = [
        (0, device * cache, cache), (cache, other + core * half, half), (cache + half, other + (1 - core) * half, half)
    ]
    for at, (left, key, count) in enumerate(stretches):
        plan_ref[places["lefts"] + at] = jnp.int32(left)
        plan_ref[places["keys"] + at] = key
        plan_ref[places["steps"] + at] = jnp.int32(count // step)
    for at in range(2 * chips):
        own = core if at < chips else 1 - core
        plan_ref[places["from"] + at] = lax.rem(chip + (chips - at % chips), chips) * 2 + own


def make_plan(shape, new_counts, prior_lengths, at):
    groups, chips = shape[:2]
    requests = new_counts.shape[0]
    sizes = dict(first_key=requests, ahead=requests, begin=requests, end=requests, side=1)
    sizes.update(groups=groups, there=groups, lefts=STRETCHES, keys=STRETCHES, steps=STRETCHES)
    sizes["from"] = 2 * chips
    places, total = {}, 0
    for name, size in sizes.items():
        places[name] = total
        total += size
    plan, far = pl.pallas_call(
        functools.partial(plan_kernel, shape, dict(places)),
        out_shape=(jax.ShapeDtypeStruct((total,), jnp.int32), jax.ShapeDtypeStruct((1,), jnp.int32)),
        in_specs=[SMEM] * 3,
        out_specs=(SMEM, SMEM),
        name="plan",
    )(new_counts, prior_lengths, at)
    return places, plan, far


def body(queries, keys, values, w_out, new_counts, prior_lengths):
    ctx_count, head_count = lax.axis_size("ctx"), lax.axis_size("head")
    rows = queries.shape[0]
    cache = keys.shape[0]
    groups, chips = ctx_count // 2, head_count // 2
    at = jnp.stack([lax.axis_index("ctx"), lax.axis_index("head")]).astype(jnp.int32)
    shape = (groups, chips, rows, cache, min(KEY_TILE, cache // 2))
    places, plan, far = make_plan(shape, new_counts, prior_lengths, at)
    requests = new_counts.shape[0]
    return lax.cond(
        far[0] == 1,
        functools.partial(attend_and_project, places, requests, True),
        functools.partial(attend_and_project, places, requests, False),
        *(queries, keys, values, w_out, plan),
    )


def attend_and_project(places, requests, far, queries, keys, values, w_out, plan):
    ctx_count, head_count = lax.axis_size("ctx"), lax.axis_size("head")
    rows = queries.shape[0]
    cache, width = keys.shape
    heads = queries.shape[1] // width
    groups, chips = ctx_count // 2, head_count // 2

    blocks = [move(queries, groups, steps, far) for steps in range(1, groups)]

    half = cache // 2
    start = lax.axis_index("head") % 2 * half
    mine = [lax.dynamic_slice_in_dim(array, start, half, axis=0) for array in (keys, values)]
    got = lax.ppermute(jnp.concatenate(mine, axis=1), "ctx", swap_pairs(ctx_count))
    all_keys, beside, own_norm, near_w = prepare(keys, values, w_out)
    stack, query_norm = stack_queries(places, plan, [queries] + blocks, width)
    got, query_norm, own_norm = lax.optimization_barrier((got, query_norm, own_norm))
    fetched = [got, lax.ppermute(got, "head", swap_pairs(head_count))]
    shape = (groups, rows, heads, requests)
    parts = attend(places, plan, (own_norm, query_norm), stack, fetched, all_keys, beside, shape)
    back = [parts[0]] + [move(parts[steps], groups, groups - steps, far) for steps in range(1, groups)]
    attended = merge(places, plan, back, heads)

    away = [lax.ppermute(attended, "head", shift_pairs(head_count, 2, steps)) for steps in range(1, chips)]
    pair = lax.ppermute(attended, "head", swap_pairs(head_count))
    mixed, token = project(places, plan, [0, chips], [attended, pair], near_w, None, False)
    away = [piece + token[0].astype(piece.dtype) for piece in away]
    away = away + [lax.ppermute(piece, "head", swap_pairs(head_count)) for piece in away]
    order = [*range(1, chips), *range(chips + 1, 2 * chips)]
    mixed, _ = project(places, plan, order, away, near_w, mixed, True)
    return mixed


def solution(mesh):
    return jax.shard_map(
        body,
        mesh=mesh,
        in_specs=(P("ctx", "head"), P("ctx", None), P("ctx", None), P(None, "head"), P(), P()),
        out_specs=P("ctx", "head"),
        check_vma=False,
    )
```

profile of v0, /device:TPU:0, one launch (start us, length us, event | category | flops | bytes accessed | tf_op | source)
XLA Modules:
  0.0 401.8 jit_solution(769351917514563768)
XLA Ops:
  0.0 0.6 pad_add_fusion.at_ref
  0.6 1.4 plan.1
  2.7 399.1 %conditional.1 = (bf16[256,4096]{1,0:T(8,128)(2,1)}) conditional(s32[]{:T(128)} %bitcast.4, (bf16[4096,128]{1,0:T(8,128)(2,1)}, bf16[4096,128]{1,0:T(8,128)(2,1)}, bf16[256,512]{1,0:T(8,128)(2,1)}, s32[54]{0:T(128)S(1)}, bf16[2048,4096]{1,0:T(8,128)(2,1)}) %tuple.13, (bf16[4096,128]{1,0:T(8,128)(2,1)}, bf16[4096,128]{1,0:T(8,128)(2,1)}, ...), branch_computations={%region_0.1_spmd, %region_1.2_spmd} | conditional | flops 17182097408 | bytes 90899152 | solution.py:529
  2.7 0.0 copy-start.5
  2.7 0.0 copy-start.1
  2.8 0.0 copy-start.3
  2.8 1.4 constant_dynamic-slice_fusion.2
  4.2 0.1 pad_maximum_fusion.1
  4.3 3.0 collective-permute-start.11
  7.3 0.0 copy-done.5
  7.3 3.6 collective-permute-start.14
  10.9 0.0 collective-permute-start.13
  10.9 1.0 collective-permute-start.12
  12.0 0.0 copy-done.1
  12.0 0.0 copy-done.3
  12.0 6.3 %prepare.3 = (bf16[8192,128]{1,0:T(8,128)(2,1)S(1)}, bf16[8192,256]{1,0:T(8,128)(2,1)S(1)}, f32[1]{0:T(128)}, bf16[2048,4096]{1,0:T(8,128)(2,1)S(1)}) custom-call(bf16[4096,128]{1,0:T(8,128)(2,1)S(1)} %copy-done.1, bf16[4096,128]{1,0:T(8,128)(2,1)S(1)} %copy-done.3, bf16[2048,4096]{1,0:T(8,128)(2,1)} %get-tuple-element.54.far_w), custom_call_target="tpu_custom_call" | custom-call | tf_op jit(solution)/shard_map/cond/branch_1_fun/prepare/pallas_call | solution.py:54
  18.3 0.0 collective-permute-done.14.refs_3_
  18.3 14.7 %collective-permute-done.13.refs_2_ = bf16[256,512]{1,0:T(8,128)(2,1)S(1)} collective-permute-done((bf16[256,512]{1,0:T(8,128)(2,1)S(1)}, bf16[256,512]{1,0:T(8,128)(2,1)S(1)}, u32[]{:S(2)}, u32[]{:S(2)}) %collective-permute-start.13) | collective-permute-done | bytes 262176 | tf_op jit(solution)/shard_map/cond/branch_1_fun/ppermute | solution.py:447
  33.0 0.0 collective-permute-done.12.refs_1_
  33.0 2.1 stack.15
  35.1 0.0 collective-permute-done.11.refs_4_
  35.1 0.1 collective-permute-start.15
  35.2 2.6 collective-permute-done.15.refs_5_
  37.8 285.7 %attend.3 = (bf16[8192,128]{1,0:T(8,128)(2,1)S(1)}, bf16[8192,256]{1,0:T(8,128)(2,1)S(1)}, bf16[272,512]{1,0:T(8,128)(2,1)S(1)}, bf16[272,512]{1,0:T(8,128)(2,1)...) custom-call(s32[54]{0:T(128)S(1)} %get-tuple-element.49.plan_ref.ref, ...), custom_call_target="tpu_custom_call", output_to_operand_aliasing={{0}: (6, {}), {1}: (7, {})} | custom-call | flops 8589934592 | bytes 25165824 | tf_op jit(solution)/shard_map/cond/branch_1_fun/attend/pallas_call | solution.py:311
  323.5 0.1 collective-permute-start.16
  323.6 37.1 %collective-permute-start.17 = (bf16[272,512]{1,0:T(8,128)(2,1)S(1)}, bf16[272,512]{1,0:T(8,128)(2,1)S(1)}, u32[]{:S(2)}, u32[]{:S(2)}) collective-permute-start(bf16[272,512]{1,0:T(8,128)(2,1)S(1)} %get-tuple-element.64), channel_id=1, source_target_pairs={{0,16},{4,20},{8,24},{12,28},{16,0},{20,4},{24,8},{28,12},{1,17},{... | collective-permute-start | bytes 835592 | tf_op jit(solution)/shard_map/cond/branch_1_fun/ppermute | solution.py:447
  360.6 0.0 collective-permute-start.18
  360.6 5.5 %collective-permute-done.16.refs_1_ = bf16[272,512]{1,0:T(8,128)(2,1)S(1)} collective-permute-done((bf16[272,512]{1,0:T(8,128)(2,1)S(1)}, bf16[272,512]{1,0:T(8,128)(2,1)S(1)}, u32[]{:S(2)}, u32[]{:S(2)}) %collective-permute-start.16) | collective-permute-done | bytes 278560 | tf_op jit(solution)/shard_map/cond/branch_1_fun/ppermute | solution.py:447
  366.1 19.1 %collective-permute-done.17.refs_2_ = bf16[272,512]{1,0:T(8,128)(2,1)S(1)} collective-permute-done((bf16[272,512]{1,0:T(8,128)(2,1)S(1)}, bf16[272,512]{1,0:T(8,128)(2,1)S(1)}, u32[]{:S(2)}, u32[]{:S(2)}) %collective-permute-start.17) | collective-permute-done | bytes 278560 | tf_op jit(solution)/shard_map/cond/branch_1_fun/ppermute | solution.py:447
  385.2 0.0 collective-permute-done.18.refs_3_
  385.2 1.8 merge.3.refs_0_
  387.0 0.1 collective-permute-start.19
  387.1 1.6 collective-permute-start.20
  388.7 0.0 collective-permute-done.19.refs_1_
  388.7 4.2 %project.6 = (f32[256,4096]{1,0:T(8,128)S(1)}, s32[1]{0:T(128)}) custom-call(s32[54]{0:T(128)S(1)} %get-tuple-element.49.plan_ref.refs_0_, bf16[256,512]{1,0:T(8,128)(2,1)S(1)} %merge.3.refs_0_, bf16[256,512]{1,0:T(8,128)(2,1)S(1)} %collective-permute-done.19.refs_1_, bf16[2048,4096]{1,0:T(8,128)(2,1)S(1)} %get-tuple-element.66.refs_2_.refs_3_), custom_call_target="tpu_custom_call" | custom-call | flops 4294967296 | bytes 16777216 | tf_op jit(solution)/shard_map/cond/branch_1_fun/project/pallas_call | solution.py:406
  393.6 2.2 collective-permute-done.20
  395.9 0.1 collective-permute-start.21
  395.9 1.5 collective-permute-done.21.refs_2_
  397.5 4.3 %project.7 = (bf16[256,4096]{1,0:T(8,128)(2,1)}, s32[1]{0:T(128)}) custom-call(s32[54]{0:T(128)S(1)} %get-tuple-element.49.plan_ref.refs_0_, f32[256,4096]{1,0:T(8,128)S(1)} %get-tuple-element.67.refs_0_, bf16[256,512]{1,0:T(8,128)(2,1)S(1)} %broadcast_add_fusion.1.refs_1_, bf16[256,512]{1,0:T(8,128)(2,1)S(1)} %collective-permute-done.21.refs_2_, ...), custom_call_target="tpu_custom_call" | custom-call | flops 4294967296 | bytes 16777216 | tf_op jit(solution)/shard_map/cond/branch_1_fun/project/pallas_call | solution.py:406
  (1 shorter events, 0.0 us)
Async XLA Ops:
  2.7 4.6 %copy-start.5 = (bf16[256,512]{1,0:T(8,128)(2,1)S(1)}, bf16[256,512]{1,0:T(8,128)(2,1)}, u32[]{:S(2)}) copy-start(bf16[256,512]{1,0:T(8,128)(2,1)} %get-tuple-element.52.refs_0_) | copy-start | bytes 786436 | tf_op jit(solution)/shard_map/cond
  2.7 9.2 %copy-start.1 = (bf16[4096,128]{1,0:T(8,128)(2,1)S(1)}, bf16[4096,128]{1,0:T(8,128)(2,1)}, u32[]{:S(2)}) copy-start(bf16[4096,128]{1,0:T(8,128)(2,1)} %get-tuple-element.50.keys_ref) | copy-start | bytes 3145732 | tf_op jit(solution)/shard_map/cond
  2.8 9.2 %copy-start.3 = (bf16[4096,128]{1,0:T(8,128)(2,1)S(1)}, bf16[4096,128]{1,0:T(8,128)(2,1)}, u32[]{:S(2)}) copy-start(bf16[4096,128]{1,0:T(8,128)(2,1)} %get-tuple-element.51.values_ref) | copy-start | bytes 3145732 | tf_op jit(solution)/shard_map/cond
  4.3 30.8 %collective-permute-start.11 = (bf16[2048,256]{1,0:T(8,128)(2,1)S(1)}, bf16[2048,256]{1,0:T(8,128)(2,1)S(1)}, u32[]{:S(2)}, u32[]{:S(2)}) collective-permute-start(bf16[2048,256]{1,0:T(8,128)(2,1)S(1)} %pad_maximum_fusion.1), channel_id=1, source_target_pairs={{0,4},{4,0},{8,12},{12,8},{16,20},{20,16},{24,28},{28,24},{1,5},{5... | collective-permute-start | bytes 3145736 | tf_op jit(solution)/shard_map/cond/branch_1_fun/ppermute | solution.py:549
  7.3 10.9 %collective-permute-start.14 = (bf16[256,512]{1,0:T(8,128)(2,1)S(1)}, bf16[256,512]{1,0:T(8,128)(2,1)S(1)}, u32[]{:S(2)}, u32[]{:S(2)}) collective-permute-start(bf16[256,512]{1,0:T(8,128)(2,1)S(1)} %copy-done.5), channel_id=1, source_target_pairs={{0,24},{4,28},{8,0},{12,4},{16,8},{20,12},{24,16},{28,20},{1,25},{... | collective-permute-start | bytes 786440 | tf_op jit(solution)/shard_map/cond/branch_1_fun/ppermute | solution.py:447
  10.9 22.0 %collective-permute-start.13 = (bf16[256,512]{1,0:T(8,128)(2,1)S(1)}, bf16[256,512]{1,0:T(8,128)(2,1)S(1)}, u32[]{:S(2)}, u32[]{:S(2)}) collective-permute-start(bf16[256,512]{1,0:T(8,128)(2,1)S(1)} %copy-done.5), channel_id=1, source_target_pairs={{0,16},{4,20},{8,24},{12,28},{16,0},{20,4},{24,8},{28,12},{1,17},{... | collective-permute-start | bytes 786440 | tf_op jit(solution)/shard_map/cond/branch_1_fun/ppermute | solution.py:447
  10.9 22.0 %collective-permute-start.12 = (bf16[256,512]{1,0:T(8,128)(2,1)S(1)}, bf16[256,512]{1,0:T(8,128)(2,1)S(1)}, u32[]{:S(2)}, u32[]{:S(2)}) collective-permute-start(bf16[256,512]{1,0:T(8,128)(2,1)S(1)} %copy-done.5), channel_id=1, source_target_pairs={{0,8},{4,12},{8,16},{12,20},{16,24},{20,28},{24,0},{28,4},{1,9},{5... | collective-permute-start | bytes 786440 | tf_op jit(solution)/shard_map/cond/branch_1_fun/ppermute | solution.py:447
  35.1 2.7 collective-permute-start.15
  323.5 42.6 %collective-permute-start.16 = (bf16[272,512]{1,0:T(8,128)(2,1)S(1)}, bf16[272,512]{1,0:T(8,128)(2,1)S(1)}, u32[]{:S(2)}, u32[]{:S(2)}) collective-permute-start(bf16[272,512]{1,0:T(8,128)(2,1)S(1)} %get-tuple-element.63), channel_id=1, source_target_pairs={{0,24},{4,28},{8,0},{12,4},{16,8},{20,12},{24,16},{28,20},{1,25},{... | collective-permute-start | bytes 835592 | tf_op jit(solution)/shard_map/cond/branch_1_fun/ppermute | solution.py:447
  323.6 61.6 %collective-permute-start.17 = (bf16[272,512]{1,0:T(8,128)(2,1)S(1)}, bf16[272,512]{1,0:T(8,128)(2,1)S(1)}, u32[]{:S(2)}, u32[]{:S(2)}) collective-permute-start(bf16[272,512]{1,0:T(8,128)(2,1)S(1)} %get-tuple-element.64), channel_id=1, source_target_pairs={{0,16},{4,20},{8,24},{12,28},{16,0},{20,4},{24,8},{28,12},{1,17},{... | collective-permute-start | bytes 835592 | tf_op jit(solution)/shard_map/cond/branch_1_fun/ppermute | solution.py:447
  360.6 24.6 %collective-permute-start.18 = (bf16[272,512]{1,0:T(8,128)(2,1)S(1)}, bf16[272,512]{1,0:T(8,128)(2,1)S(1)}, u32[]{:S(2)}, u32[]{:S(2)}) collective-permute-start(bf16[272,512]{1,0:T(8,128)(2,1)S(1)} %get-tuple-element.65), channel_id=1, source_target_pairs={{0,8},{4,12},{8,16},{12,20},{16,24},{20,28},{24,0},{28,4},{1,9},{5... | collective-permute-start | bytes 835592 | tf_op jit(solution)/shard_map/cond/branch_1_fun/ppermute | solution.py:447
  387.0 1.7 collective-permute-start.19
  387.1 8.7 %collective-permute-start.20 = (bf16[256,512]{1,0:T(8,128)(2,1)S(1)}, bf16[256,512]{1,0:T(8,128)(2,1)S(1)}, u32[]{:S(2)}, u32[]{:S(2)}) collective-permute-start(bf16[256,512]{1,0:T(8,128)(2,1)S(1)} %merge.3.refs_0_), channel_id=1, source_target_pairs={{0,2},{1,3},{2,0},{3,1},{4,6},{5,7},{6,4},{7,5},{8,10},{9,11},{10,... | collective-permute-start | bytes 786440 | tf_op jit(solution)/shard_map/cond/branch_1_fun/ppermute | solution.py:559
  395.9 1.6 collective-permute-start.21
where the time goes:
time: 402 us
  Pallas kernels  306 us (76%)
  starting transfers between devices  46.5 us (12%)
  waiting for transfers between devices  45.7 us (11%)
    pallas_call x1, Pallas kernels, attend(): pl.pallas_call(functools.partial(attend_kernel, shape, dict(places)), out...  286 us
    ppermute x6, starting transfers between devices, move(): return lax.ppermute(value, 'ctx', pairs) if pairs else jnp.zeros_like(value)  41.7 us
    ppermute x6, waiting for transfers between devices, move(): return lax.ppermute(value, 'ctx', pairs) if pairs else jnp.zeros_like(value)  39.3 us
    pallas_call x2, Pallas kernels, project(): pl.pallas_call(functools.partial(project_kernel, order, going_on, last, p...  8.55 us
  transfers between devices with their start and end apart: 11, of which 6 were waited for; matrix products, arithmetic and copies ran while one was open for 0% of the time, Pallas kernels for 3%

commit v1 on v0

--- a/solution.py
+++ b/solution.py
@@ -67,7 +67,8 @@
     )(keys, values, pltpu.with_memory_space_constraint(w_out, pltpu.HBM))
 
 
-def stack_kernel(slots, group_at, width, plan_ref, *refs):
+def stack_kernel(order, group_at, width, plan_ref, *refs):
+    slots = len(order)
     q_refs, (stack_ref, longest_ref, q_all, sems) = refs[:slots], refs[slots:]
     rows = q_refs[0].shape[0]
     heads = q_refs[0].shape[1] // width
@@ -78,7 +79,7 @@
     longest = jnp.zeros((rows, 1), jnp.float32)
     for slot, copy in enumerate(copies):
         copy.wait()
-        start = plan_ref[group_at + slot] * rows
+        start = plan_ref[group_at + order[slot]] * rows
         for head in range(heads):
             part = q_all[slot, :, head * width:(head + 1) * width]
             stack_ref[pl.ds(pl.multiple_of(head * local + start, rows), rows), :] = part
@@ -86,10 +87,10 @@
     longest_ref[0] = jnp.max(longest)
 
 
-def stack_queries(places, plan, queries, width):
+def stack_queries(places, plan, order, queries, width):
     slots, (rows, wide) = len(queries), queries[0].shape
     return pl.pallas_call(
-        functools.partial(stack_kernel, slots, places["groups"], width),
+        functools.partial(stack_kernel, order, places["groups"], width),
         out_shape=(
             pltpu.VMEM((slots * rows * (wide // width), width), jnp.bfloat16),
             jax.ShapeDtypeStruct((1,), jnp.float32),
@@ -333,12 +334,12 @@
     return payloads
 
 
-def merge_kernel(heads, there_at, plan_ref, *refs):
+def merge_kernel(heads, order, there_at, plan_ref, *refs):
     parts, out_ref = refs[:-1], refs[-1]
     rows = out_ref.shape[0]
     width = out_ref.shape[1] // heads
     logs = [
-        jnp.where(plan_ref[there_at + at] == 1, part[rows:, :rows].astype(jnp.float32), 0.0) for at, part in enumerate(parts)
+        jnp.where(plan_ref[there_at + order[at]] == 1, part[rows:, :rows].astype(jnp.float32), 0.0) for at, part in enumerate(parts)
     ]
     spare = LANES - SIDE * len(parts)
     if spare:
@@ -366,10 +367,10 @@
         out_ref[:, own] = mixed.astype(out_ref.dtype)
 
 
-def merge(places, plan, parts, heads):
+def merge(places, plan, order, parts, heads):
     rows = parts[0].shape[0] - SIDE
     return pl.pallas_call(
-        functools.partial(merge_kernel, heads, places["there"]),
+        functools.partial(merge_kernel, heads, order, places["there"]),
         out_shape=jax.ShapeDtypeStruct((rows, parts[0].shape[1]), jnp.bfloat16),
         in_specs=[SMEM] + [VMEM] * len(parts),
         out_specs=VMEM,
@@ -447,10 +448,18 @@
     return lax.ppermute(value, "ctx", pairs) if pairs else jnp.zeros_like(value)
 
 
-def plan_kernel(shape, places, new_ref, prior_ref, at_ref, plan_ref, far_ref):
+def plan_kernel(shape, places, new_ref, prior_ref, at_ref, keys_ref, values_ref, plan_ref, far_ref, mine_ref, sems):
     groups, chips, rows, cache, step = shape
     device, place = at_ref[0], at_ref[1]
     group, side, chip, core = lax.div(device, 2), lax.rem(device, 2), lax.div(place, 2), lax.rem(place, 2)
+    half, width = mine_ref.shape[0], keys_ref.shape[1]
+    here = pl.ds(pl.multiple_of(core * half, half), half)
+    copies = [
+        pltpu.make_async_copy(ref.at[here, :], mine_ref.at[:, at * width:(at + 1) * width], sems.at[at])
+        for at, ref in enumerate((keys_ref, values_ref))
+    ]
+    for copy in copies:
+        copy.start()
     table = request_table(new_ref, prior_ref)
 
     def rows_before(row):
@@ -495,9 +504,11 @@
     for at in range(2 * chips):
         own = core if at < chips else 1 - core
         plan_ref[places["from"] + at] = lax.rem(chip + (chips - at % chips), chips) * 2 + own
-
-
-def make_plan(shape, new_counts, prior_lengths, at):
+    for copy in copies:
+        copy.wait()
+
+
+def make_plan(shape, new_counts, prior_lengths, at, keys, values):
     groups, chips = shape[:2]
     requests = new_counts.shape[0]
     sizes = dict(first_key=requests, ahead=requests, begin=requests, end=requests, side=1)
@@ -507,14 +518,19 @@
     for name, size in sizes.items():
         places[name] = total
         total += size
-    plan, far = pl.pallas_call(
+    plan, far, mine = pl.pallas_call(
         functools.partial(plan_kernel, shape, dict(places)),
-        out_shape=(jax.ShapeDtypeStruct((total,), jnp.int32), jax.ShapeDtypeStruct((1,), jnp.int32)),
-        in_specs=[SMEM] * 3,
-        out_specs=(SMEM, SMEM),
+        out_shape=(
+            jax.ShapeDtypeStruct((total,), jnp.int32),
+            jax.ShapeDtypeStruct((1,), jnp.int32),
+            pltpu.HBM((keys.shape[0] // 2, 2 * keys.shape[1]), keys.dtype),
+        ),
+        in_specs=[SMEM] * 3 + [HBM] * 2,
+        out_specs=(SMEM, SMEM, HBM),
+        scratch_shapes=[pltpu.SemaphoreType.DMA((2,))],
         name="plan",
-    )(new_counts, prior_lengths, at)
-    return places, plan, far
+    )(new_counts, prior_lengths, at, keys, values)
+    return places, plan, far, mine
 
 
 def body(queries, keys, values, w_out, new_counts, prior_lengths):
@@ -524,37 +540,35 @@
     groups, chips = ctx_count // 2, head_count // 2
     at = jnp.stack([lax.axis_index("ctx"), lax.axis_index("head")]).astype(jnp.int32)
     shape = (groups, chips, rows, cache, min(KEY_TILE, cache // 2))
-    places, plan, far = make_plan(shape, new_counts, prior_lengths, at)
+    places, plan, far, mine = make_plan(shape, new_counts, prior_lengths, at, keys, values)
     requests = new_counts.shape[0]
     return lax.cond(
         far[0] == 1,
         functools.partial(attend_and_project, places, requests, True),
         functools.partial(attend_and_project, places, requests, False),
-        *(queries, keys, values, w_out, plan),
+        *(queries, keys, values, w_out, plan, mine),
     )
 
 
-def attend_and_project(places, requests, far, queries, keys, values, w_out, plan):
+def attend_and_project(places, requests, far, queries, keys, values, w_out, plan, mine):
     ctx_count, head_count = lax.axis_size("ctx"), lax.axis_size("head")
     rows = queries.shape[0]
     cache, width = keys.shape
     heads = queries.shape[1] // width
     groups, chips = ctx_count // 2, head_count // 2
 
-    blocks = [move(queries, groups, steps, far) for steps in range(1, groups)]
-
-    half = cache // 2
-    start = lax.axis_index("head") % 2 * half
-    mine = [lax.dynamic_slice_in_dim(array, start, half, axis=0) for array in (keys, values)]
-    got = lax.ppermute(jnp.concatenate(mine, axis=1), "ctx", swap_pairs(ctx_count))
+    nearest = sorted(range(1, groups), key=lambda steps: min(steps, groups - steps))
+    blocks = [move(queries, groups, steps, far) for steps in reversed(nearest)]
+
+    got = lax.ppermute(mine, "ctx", swap_pairs(ctx_count))
     all_keys, beside, own_norm, near_w = prepare(keys, values, w_out)
-    stack, query_norm = stack_queries(places, plan, [queries] + blocks, width)
+    stack, query_norm = stack_queries(places, plan, [0, *reversed(nearest)], [queries] + blocks, width)
     got, query_norm, own_norm = lax.optimization_barrier((got, query_norm, own_norm))
     fetched = [got, lax.ppermute(got, "head", swap_pairs(head_count))]
     shape = (groups, rows, heads, requests)
     parts = attend(places, plan, (own_norm, query_norm), stack, fetched, all_keys, beside, shape)
-    back = [parts[0]] + [move(parts[steps], groups, groups - steps, far) for steps in range(1, groups)]
-    attended = merge(places, plan, back, heads)
+    back = [parts[0]] + [move(parts[steps], groups, groups - steps, far) for steps in nearest]
+    attended = merge(places, plan, [0, *nearest], back, heads)
 
     away = [lax.ppermute(attended, "head", shift_pairs(head_count, 2, steps)) for steps in range(1, chips)]
     pair = lax.ppermute(attended, "head", swap_pairs(head_count))

time: 402 us -> 426 us (1.060)
  Pallas kernels: 306 us -> 360 us
  starting transfers between devices: 46.5 us -> 25.1 us
  waiting for transfers between devices: 45.7 us -> 39.2 us
    pallas_call x1, Pallas kernels: 1.42 us -> 34.2 us  [make_plan(): pl.pallas_call(functools.partial(plan_kernel, shape, dict(places)), out_s...]
    ppermute x6, starting transfers between devices: 41.7 us -> 20.3 us  [move(): return lax.ppermute(value, 'ctx', pairs) if pairs else jnp.zeros_like(value)]
    pallas_call x1, Pallas kernels: 286 us -> 305 us  [attend(): pl.pallas_call(functools.partial(attend_kernel, shape, dict(places)), out...]
    ppermute x6, waiting for transfers between devices: 39.3 us -> 32.8 us  [move(): return lax.ppermute(value, 'ctx', pairs) if pairs else jnp.zeros_like(value)]
  transfers between devices with their start and end apart: 11 -> 11, of which waited for: 6 -> 8; matrix products, arithmetic and copies ran while one was open for 0% -> 0% of each run, Pallas kernels for 3% -> 3%
where the time goes in v1:
time: 426 us
  Pallas kernels  360 us (85%)
  waiting for transfers between devices  39.2 us (9%)
  starting transfers between devices  25.1 us (6%)
    pallas_call x1, Pallas kernels, attend(): pl.pallas_call(functools.partial(attend_kernel, shape, dict(places)), out...  305 us
    pallas_call x1, Pallas kernels, make_plan(): pl.pallas_call(functools.partial(plan_kernel, shape, dict(places)), out_s...  34.2 us
    ppermute x6, waiting for transfers between devices, move(): return lax.ppermute(value, 'ctx', pairs) if pairs else jnp.zeros_like(value)  32.8 us
    ppermute x6, starting transfers between devices, move(): return lax.ppermute(value, 'ctx', pairs) if pairs else jnp.zeros_like(value)  20.3 us
    pallas_call x2, Pallas kernels, project(): pl.pallas_call(functools.partial(project_kernel, order, going_on, last, p...  8.55 us
  transfers between devices with their start and end apart: 11, of which 8 were waited for; matrix products, arithmetic and copies ran while one was open for 0% of the time, Pallas kernels for 3%

profile of v1, /device:TPU:0, one launch (start us, length us, event | category | flops | bytes accessed | tf_op | source)
XLA Modules:
  0.0 425.9 jit_solution(18263553720618696833)
XLA Ops:
  0.0 0.7 pad_add_fusion.at_ref
  0.7 34.2 %plan.1 = (s32[54]{0:T(128)S(1)}, s32[1]{0:T(128)}, bf16[2048,256]{1,0:T(8,128)(2,1)}) custom-call(s32[8]{0:T(128)} %new_ref.1, s32[8]{0:T(128)} %prior_ref.1, s32[2]{0:T(128)} %pad_add_fusion.at_ref, bf16[4096,128]{1,0:T(8,128)(2,1)} %keys_ref.1, bf16[4096,128]{1,0:T(8,128)(2,1)} %values_ref.1), custom_call_target="tpu_custom_call" | custom-call | tf_op jit(solution)/shard_map/plan/pallas_call | solution.py:521
  35.5 390.4 %conditional.1 = (bf16[256,4096]{1,0:T(8,128)(2,1)}) conditional(s32[]{:T(128)} %bitcast.4, (bf16[2048,256]{1,0:T(8,128)(2,1)}, bf16[256,512]{1,0:T(8,128)(2,1)}, s32[54]{0:T(128)S(1)}, bf16[4096,128]{1,0:T(8,128)(2,1)}, bf16[4096,128]{1,0:T(8,128)(2,1)}, /*index=5*/bf16[2048,4096]{1,0:T(8,128)(2,1)}) %tuple.13, (bf16[2048,256]{1,0:T(8,128)(2,1)}, ...), branch_computations={%region_0.0_spmd, %region_1.0_spmd} | conditional | flops 17180000256 | bytes 78316000 | solution.py:545
  35.5 3.0 collective-permute-start.11
  38.5 1.6 collective-permute-start.14
  40.1 2.2 collective-permute-start.13
  42.3 0.8 collective-permute-start.12
  43.1 0.0 copy-start.1
  43.1 7.9 %prepare.3 = (bf16[8192,128]{1,0:T(8,128)(2,1)S(1)}, bf16[8192,256]{1,0:T(8,128)(2,1)S(1)}, f32[1]{0:T(128)}, bf16[2048,4096]{1,0:T(8,128)(2,1)S(1)}) custom-call(bf16[4096,128]{1,0:T(8,128)(2,1)} %get-tuple-element.58.keys_ref, bf16[4096,128]{1,0:T(8,128)(2,1)} %get-tuple-element.59.values_ref, bf16[2048,4096]{1,0:T(8,128)(2,1)} %get-tuple-element.60.far_w), custom_call_target="tpu_custom_call" | custom-call | tf_op jit(solution)/shard_map/cond/branch_1_fun/prepare/pallas_call | solution.py:54
  51.0 0.0 collective-permute-done.14.refs_3_
  51.0 2.4 collective-permute-done.13.refs_2_
  53.4 11.8 %collective-permute-done.12.refs_1_ = bf16[256,512]{1,0:T(8,128)(2,1)S(1)} collective-permute-done((bf16[256,512]{1,0:T(8,128)(2,1)}, bf16[256,512]{1,0:T(8,128)(2,1)S(1)}, u32[]{:S(2)}, u32[]{:S(2)}) %collective-permute-start.12) | collective-permute-done | bytes 262176 | tf_op jit(solution)/shard_map/cond/branch_1_fun/ppermute | solution.py:448
  65.2 0.0 copy-done.1
  65.2 2.1 stack.15
  67.3 0.0 collective-permute-done.11.refs_4_
  67.3 0.1 collective-permute-start.15
  67.4 2.6 collective-permute-done.15.refs_5_
  70.1 305.0 %attend.3 = (bf16[8192,128]{1,0:T(8,128)(2,1)S(1)}, bf16[8192,256]{1,0:T(8,128)(2,1)S(1)}, bf16[272,512]{1,0:T(8,128)(2,1)S(1)}, bf16[272,512]{1,0:T(8,128)(2,1)...) custom-call(s32[54]{0:T(128)S(1)} %get-tuple-element.54.plan_ref.ref, ...), custom_call_target="tpu_custom_call", output_to_operand_aliasing={{0}: (6, {}), {1}: (7, {})} | custom-call | flops 8589934592 | bytes 25165824 | tf_op jit(solution)/shard_map/cond/branch_1_fun/attend/pallas_call | solution.py:312
  375.1 0.1 collective-permute-start.16
  375.2 14.2 %collective-permute-start.17 = (bf16[272,512]{1,0:T(8,128)(2,1)S(1)}, bf16[272,512]{1,0:T(8,128)(2,1)S(1)}, u32[]{:S(2)}, u32[]{:S(2)}) collective-permute-start(bf16[272,512]{1,0:T(8,128)(2,1)S(1)} %get-tuple-element.70), channel_id=1, source_target_pairs={{0,8},{4,12},{8,16},{12,20},{16,24},{20,28},{24,0},{28,4},{1,9},{5... | collective-permute-start | bytes 835592 | tf_op jit(solution)/shard_map/cond/branch_1_fun/ppermute | solution.py:448
  389.4 1.4 collective-permute-start.18
  390.8 5.5 %collective-permute-done.16.refs_1_ = bf16[272,512]{1,0:T(8,128)(2,1)S(1)} collective-permute-done((bf16[272,512]{1,0:T(8,128)(2,1)S(1)}, bf16[272,512]{1,0:T(8,128)(2,1)S(1)}, u32[]{:S(2)}, u32[]{:S(2)}) %collective-permute-start.16) | collective-permute-done | bytes 278560 | tf_op jit(solution)/shard_map/cond/branch_1_fun/ppermute | solution.py:448
  396.3 0.1 collective-permute-done.17.refs_2_
  396.4 13.0 %collective-permute-done.18.refs_3_ = bf16[272,512]{1,0:T(8,128)(2,1)S(1)} collective-permute-done((bf16[272,512]{1,0:T(8,128)(2,1)S(1)}, bf16[272,512]{1,0:T(8,128)(2,1)S(1)}, u32[]{:S(2)}, u32[]{:S(2)}) %collective-permute-start.18) | collective-permute-done | bytes 278560 | tf_op jit(solution)/shard_map/cond/branch_1_fun/ppermute | solution.py:448
  409.4 1.8 merge.3.refs_0_
  411.2 0.1 collective-permute-start.19
  411.3 1.6 collective-permute-start.20
  412.8 0.0 collective-permute-done.19.refs_1_
  412.8 4.2 project.6
  417.7 2.2 collective-permute-done.20
  420.0 0.1 collective-permute-start.21
  420.1 1.5 collective-permute-done.21.refs_2_
  421.6 4.3 %project.7 = (bf16[256,4096]{1,0:T(8,128)(2,1)}, s32[1]{0:T(128)}) custom-call(s32[54]{0:T(128)S(1)} %get-tuple-element.54.plan_ref.refs_0_, f32[256,4096]{1,0:T(8,128)S(1)} %get-tuple-element.73.refs_0_, bf16[256,512]{1,0:T(8,128)(2,1)S(1)} %broadcast_add_fusion.1.refs_1_, bf16[256,512]{1,0:T(8,128)(2,1)S(1)} %collective-permute-done.21.refs_2_, ...), custom_call_target="tpu_custom_call" | custom-call | flops 4294967296 | bytes 16777216 | tf_op jit(solution)/shard_map/cond/branch_1_fun/project/pallas_call | solution.py:407
  (1 shorter events, 0.0 us)
Async XLA Ops:
  35.5 31.8 %collective-permute-start.11 = (bf16[2048,256]{1,0:T(8,128)(2,1)}, bf16[2048,256]{1,0:T(8,128)(2,1)S(1)}, u32[]{:S(2)}, u32[]{:S(2)}) collective-permute-start(bf16[2048,256]{1,0:T(8,128)(2,1)} %get-tuple-element.55), channel_id=1, source_target_pairs={{0,4},{4,0},{8,12},{12,8},{16,20},{20,16},{24,28},{28,24},{1,5},{5... | collective-permute-start | bytes 3145736 | tf_op jit(solution)/shard_map/cond/branch_1_fun/ppermute | solution.py:563
  38.5 12.5 %collective-permute-start.14 = (bf16[256,512]{1,0:T(8,128)(2,1)}, bf16[256,512]{1,0:T(8,128)(2,1)S(1)}, u32[]{:S(2)}, u32[]{:S(2)}) collective-permute-start(bf16[256,512]{1,0:T(8,128)(2,1)} %get-tuple-element.56.refs_0_), channel_id=1, source_target_pairs={{0,8},{4,12},{8,16},{12,20},{16,24},{20,28},{24,0},{28,4},{1,9},{5... | collective-permute-start | bytes 786440 | tf_op jit(solution)/shard_map/cond/branch_1_fun/ppermute | solution.py:448
  40.1 13.3 %collective-permute-start.13 = (bf16[256,512]{1,0:T(8,128)(2,1)}, bf16[256,512]{1,0:T(8,128)(2,1)S(1)}, u32[]{:S(2)}, u32[]{:S(2)}) collective-permute-start(bf16[256,512]{1,0:T(8,128)(2,1)} %get-tuple-element.56.refs_0_), channel_id=1, source_target_pairs={{0,24},{4,28},{8,0},{12,4},{16,8},{20,12},{24,16},{28,20},{1,25},{... | collective-permute-start | bytes 786440 | tf_op jit(solution)/shard_map/cond/branch_1_fun/ppermute | solution.py:448
  42.3 22.9 %collective-permute-start.12 = (bf16[256,512]{1,0:T(8,128)(2,1)}, bf16[256,512]{1,0:T(8,128)(2,1)S(1)}, u32[]{:S(2)}, u32[]{:S(2)}) collective-permute-start(bf16[256,512]{1,0:T(8,128)(2,1)} %get-tuple-element.56.refs_0_), channel_id=1, source_target_pairs={{0,16},{4,20},{8,24},{12,28},{16,0},{20,4},{24,8},{28,12},{1,17},{... | collective-permute-start | bytes 786440 | tf_op jit(solution)/shard_map/cond/branch_1_fun/ppermute | solution.py:448
  43.1 22.1 %copy-start.1 = (bf16[256,512]{1,0:T(8,128)(2,1)S(1)}, bf16[256,512]{1,0:T(8,128)(2,1)}, u32[]{:S(2)}) copy-start(bf16[256,512]{1,0:T(8,128)(2,1)} %get-tuple-element.56.refs_0_) | copy-start | bytes 786436 | tf_op jit(solution)/shard_map/cond
  67.3 2.7 collective-permute-start.15
  375.1 21.1 %collective-permute-start.16 = (bf16[272,512]{1,0:T(8,128)(2,1)S(1)}, bf16[272,512]{1,0:T(8,128)(2,1)S(1)}, u32[]{:S(2)}, u32[]{:S(2)}) collective-permute-start(bf16[272,512]{1,0:T(8,128)(2,1)S(1)} %get-tuple-element.69), channel_id=1, source_target_pairs={{0,24},{4,28},{8,0},{12,4},{16,8},{20,12},{24,16},{28,20},{1,25},{... | collective-permute-start | bytes 835592 | tf_op jit(solution)/shard_map/cond/branch_1_fun/ppermute | solution.py:448
  375.2 21.2 %collective-permute-start.17 = (bf16[272,512]{1,0:T(8,128)(2,1)S(1)}, bf16[272,512]{1,0:T(8,128)(2,1)S(1)}, u32[]{:S(2)}, u32[]{:S(2)}) collective-permute-start(bf16[272,512]{1,0:T(8,128)(2,1)S(1)} %get-tuple-element.70), channel_id=1, source_target_pairs={{0,8},{4,12},{8,16},{12,20},{16,24},{20,28},{24,0},{28,4},{1,9},{5... | collective-permute-start | bytes 835592 | tf_op jit(solution)/shard_map/cond/branch_1_fun/ppermute | solution.py:448
  389.4 20.0 %collective-permute-start.18 = (bf16[272,512]{1,0:T(8,128)(2,1)S(1)}, bf16[272,512]{1,0:T(8,128)(2,1)S(1)}, u32[]{:S(2)}, u32[]{:S(2)}) collective-permute-start(bf16[272,512]{1,0:T(8,128)(2,1)S(1)} %get-tuple-element.71), channel_id=1, source_target_pairs={{0,16},{4,20},{8,24},{12,28},{16,0},{20,4},{24,8},{28,12},{1,17},{... | collective-permute-start | bytes 835592 | tf_op jit(solution)/shard_map/cond/branch_1_fun/ppermute | solution.py:448
  411.2 1.7 collective-permute-start.19
  411.3 8.7 %collective-permute-start.20 = (bf16[256,512]{1,0:T(8,128)(2,1)S(1)}, bf16[256,512]{1,0:T(8,128)(2,1)S(1)}, u32[]{:S(2)}, u32[]{:S(2)}) collective-permute-start(bf16[256,512]{1,0:T(8,128)(2,1)S(1)} %merge.3.refs_0_), channel_id=1, source_target_pairs={{0,2},{1,3},{2,0},{3,1},{4,6},{5,7},{6,4},{7,5},{8,10},{9,11},{10,... | collective-permute-start | bytes 786440 | tf_op jit(solution)/shard_map/cond/branch_1_fun/ppermute | solution.py:573
  420.0 1.6 collective-permute-start.21
